TPU v7x, 512 devices: a whole 4x4x16 slice. The times are simulated.
512 devices in a mesh: query: 32 (over y, x, core), passage: 16 (over z).
Axes of the slice: x: 4, y: 4, z: 16, core: 2. Of those that a mesh axis runs over, the one named last changes fastest.
Arguments:
- queries: bfloat16 [4096, 4096], P('query'), may hold values from -12 to 12
- cand_ids: int32 [4096, 128], P('query'), may hold values from 0 to 2047, all different within a row
- teacher: int32 [4096, 128], P('query'), may hold values from 0 to 2047
- hidden_states: bfloat16 [2048, 4096], P('passage', 'query'), may hold values from -6 to 6
- gain: bfloat16 [4096], P('query'), may hold values from 0.5 to 1.5
Outputs:
- q_grad: bfloat16 [4096, 4096], P('query', 'passage')
- h_grad: bfloat16 [2048, 4096], P('passage', 'query')
- gain_grad: float32 [4096], P('query')
Inputs may be any that keep to these rules, and one draw needn't show every extreme that they name: `cand_ids`: each query lists 128 different passages; every passage is listed by some query.
All inputs are finite; a program needn't handle non-finite values.
Results may differ from a plain program's by a relative error of at most 0.012.
The roundings to bfloat16 on the way count: a program that leaves them out, or rounds other values in their place, can miss the bound.
Values may be sent and summed in bfloat16 or wider, within the bound.
A program may use at most 64 MiB of HBM per device.

v0:
```python
import jax
import jax.numpy as jnp
from jax import lax
from jax.sharding import PartitionSpec as P

D = 4096


def shards(queries, cand_ids, teacher, hidden_states, gain):
    full_hidden, gain_full = (
        lax.all_gather(hidden_states, "query", axis=1, tiled=True),
        lax.all_gather(gain, "query", axis=0, tiled=True),
    )
    owned_rows = full_hidden.shape[0]
    hidden_rows = full_hidden.astype(jnp.float32)
    inv_rms = lax.rsqrt(jnp.mean(hidden_rows * hidden_rows, axis=1) + 1e-05)
    embedded = (hidden_rows * inv_rms[:, None] * gain_full.astype(jnp.float32)).astype(jnp.bfloat16)
    score_scale = float(D) ** (-0.5)
    dense_scores = (
        lax.dot_general(
            queries, embedded, (((1,), (1,)), ((), ())), preferred_element_type=jnp.float32
        )
        * score_scale
    )
    offset = lax.axis_index("passage") * owned_rows
    local_index = cand_ids - offset
    is_owned = (local_index >= 0) & (local_index < owned_rows)
    owner_iota = lax.broadcasted_iota(jnp.int32, (1, 1, owned_rows), 2)
    matches = local_index[:, :, None] == owner_iota
    scores = jnp.sum(jnp.where(matches, dense_scores[:, None, :], 0.0), axis=2)
    masked = jnp.where(is_owned, scores, -1e30)
    top_score = lax.pmax(jnp.max(masked, axis=1), "passage")
    totals = lax.psum(
        jnp.sum(jnp.where(is_owned, jnp.exp(masked - top_score[:, None]), 0.0), axis=1), "passage"
    )
    student = jnp.exp(masked - top_score[:, None]) / totals[:, None]
    target = jax.nn.softmax(teacher.astype(jnp.float32) * 0.125, axis=1)
    list_grad = jnp.where(is_owned, student - target, 0.0)
    grad_table = jnp.sum(jnp.where(matches, list_grad[:, :, None], 0.0), axis=1).astype(
        jnp.bfloat16
    )
    query_part = jnp.dot(grad_table, embedded, preferred_element_type=jnp.float32)
    q_grad = lax.psum_scatter(query_part, "passage", scatter_dimension=1, tiled=True).astype(
        jnp.bfloat16
    )
    partial_grads = lax.dot_general(
        grad_table, queries, (((0,), (0,)), ((), ())), preferred_element_type=jnp.float32
    )
    e_slice = lax.psum_scatter(partial_grads, "query", scatter_dimension=1, tiled=True)
    hidden_slice = hidden_states.astype(jnp.float32)
    scaled = e_slice * gain.astype(jnp.float32)
    row_mean = lax.psum(jnp.sum(scaled * hidden_slice, axis=1), "query") / float(D)
    h_grad = (
        inv_rms[:, None] * scaled - hidden_slice * (inv_rms**3)[:, None] * row_mean[:, None]
    ).astype(jnp.bfloat16)
    gain_grad = lax.psum(jnp.sum(e_slice * hidden_slice * inv_rms[:, None], axis=0), "passage")
    return (q_grad, h_grad, gain_grad)


def solution(mesh):
    placed = (
        P("query", None),
        P("query", None),
        P("query", None),
        P("passage", "query"),
        P("query"),
    )
    return jax.shard_map(
        shards,
        mesh=mesh,
        in_specs=placed,
        out_specs=(P("query", "passage"), P("passage", "query"), P("query")),
        check_vma=False,
    )
```

profile of v0, /device:TPU:1, one launch (start us, length us, event | category | flops | bytes accessed | tf_op | source)
XLA Modules:
  0.0 347.3 jit_solution(17466982796609698326)
XLA Ops:
  7.2 0.0 copy-start
  7.2 0.0 all-gather.3.cloned.1.call-start
  7.2 0.7 all-gather.3.cloned.1.call-update
  7.9 0.0 reduce-scatter.5.cloned.1.call-start
  8.0 24.1 %all-gather = bf16[32,1,128]{2,1,0:T(2,128)(2,1)S(1)} all-gather(bf16[1,1,128]{2,1,0:T(2,128)(2,1)} %bitcast.10), channel_id=1, replica_groups=mesh['query'=32,'passage'=16] {'query'}, dimensions={0}, use_global_device_ids=true | all-gather | bytes 8448 | tf_op jit(solution)/shard_map/all_gather | solution.py:12
  32.0 0.9 fusion.13
  33.0 1.0 fusion.14
  34.0 0.9 broadcast_subtract_fusion
  34.9 0.0 copy-start.4
  34.9 0.0 copy-start.2
  34.9 40.2 %all-gather.3.cloned.1.call-done = bf16[128,4096]{1,0:T(8,128)(2,1)} async-done(((bf16[128,128]{1,0:T(8,128)(2,1)}), bf16[128,4096]{1,0:T(8,128)(2,1)}) %all-gather.3.cloned.1.call-update) | async-done | bytes 1048592 | tf_op jit(solution)/shard_map/all_gather | solution.py:11
  75.1 1.5 fusion
  76.6 0.0 copy-done
  76.6 1.7 fusion.3
  78.4 0.1 copy.10
  78.5 5.1 %select_reduce_fusion.1 = f32[128,128]{1,0:T(8,128)S(1)} fusion(f32[128,128]{1,0:T(8,128)S(1)} %copy.10, s32[128,128]{1,0:T(8,128)S(1)} %broadcast_subtract_fusion), kind=kLoop, calls=%fused_computation.1 | loop fusion | flops 6275072 | bytes 196608 | tf_op jit(solution)/shard_map/reduce_sum | solution.py:30
  83.6 0.0 copy-done.4
  83.6 0.1 fusion.15
  83.7 24.7 %pmax.7 = f32[128]{0:T(128)S(1)} all-reduce(f32[128]{0:T(128)S(1)} %get-tuple-element.5), channel_id=1, replica_groups=mesh['query'=32,'passage'=16] {'passage'}, use_global_device_ids=true, to_apply=%region_3.4 | all-reduce | flops 128 | bytes 1024 | tf_op jit(solution)/shard_map/pmax | solution.py:32
  108.5 0.2 select_reduce_fusion.2
  108.6 21.0 %psum.21 = f32[128]{0:T(128)S(1)} all-reduce(f32[128]{0:T(128)S(1)} %select_reduce_fusion.2), channel_id=1, replica_groups=mesh['query'=32,'passage'=16] {'passage'}, use_global_device_ids=true, to_apply=%region_5.6 | all-reduce | flops 128 | bytes 1024 | tf_op jit(solution)/shard_map/psum | solution.py:33
  129.7 0.0 copy-done.2
  129.7 0.1 subtract_select_fusion
  129.8 5.6 %select_reduce_fusion = bf16[128,128]{1,0:T(8,128)(2,1)S(1)} fusion(f32[128,128]{1,0:T(8,128)S(1)} %subtract_select_fusion, s32[128,128]{1,0:T(8,128)S(1)} %broadcast_subtract_fusion), kind=kLoop, calls=%fused_computation | loop fusion | flops 6275072 | bytes 163840 | tf_op jit(solution)/shard_map/reduce_sum | solution.py:39
  135.4 0.0 copy-start.1
  135.4 1.8 fusion.19
  137.3 0.0 reduce-scatter.5.cloned.1.call-update
  137.3 0.0 copy-start.5
  137.3 0.0 copy-start.3
  137.3 0.0 reduce-scatter.3.cloned.1.call-start
  137.4 0.0 copy-done.1
  137.4 1.8 fusion.4
  139.2 0.0 reduce-scatter.3.cloned.1.call-update
  139.2 0.0 copy-done.5
  139.2 107.8 %reduce-scatter.5.cloned.1.call-done = f32[128,128]{1,0:T(8,128)} async-done(((f32[128,4096]{1,0:T(8,128)}), f32[128,128]{1,0:T(8,128)}) %reduce-scatter.5.cloned.1.call-update) | async-done | bytes 65552 | tf_op jit(solution)/shard_map/reduce_scatter | solution.py:49
  247.0 0.0 copy-done.3
  247.1 1.0 fusion.12
  248.0 64.3 %psum.22 = f32[128]{0:T(128)S(1)} all-reduce(f32[128]{0:T(128)S(1)} %get-tuple-element.4), channel_id=1, replica_groups=mesh['query'=32,'passage'=16] {'query'}, use_global_device_ids=true, to_apply=%region_12.13 | all-reduce | flops 128 | bytes 1024 | tf_op jit(solution)/shard_map/psum | solution.py:52
  312.3 25.4 %psum.23 = f32[128]{0:T(128)} all-reduce(f32[128]{0:T(128)S(1)} %get-tuple-element.3), channel_id=1, replica_groups=mesh['query'=32,'passage'=16] {'passage'}, use_global_device_ids=true, to_apply=%region_14.15 | all-reduce | flops 128 | bytes 1024 | tf_op jit(solution)/shard_map/psum | solution.py:56
  337.7 1.6 fusion.9
  339.3 0.0 reduce-scatter.3.cloned.1.call-done
  339.3 1.5 convert_element_type.32
  (4 shorter events, 0.0 us)
Async XLA Ops:
  7.2 69.5 %copy-start = (bf16[128,4096]{1,0:T(8,128)(2,1)S(1)}, bf16[128,4096]{1,0:T(8,128)(2,1)}, u32[]{:S(2)}) copy-start(bf16[128,4096]{1,0:T(8,128)(2,1)} %param.5) | copy-start | bytes 3145732
  7.2 67.9 %all-gather.3.cloned.1.call-start = ((), (), s32[]{:S(2)}) async-start(), calls=%async_computation.2 | async-start | bytes 1081344 | tf_op jit(solution)/shard_map/all_gather | solution.py:11
  7.9 239.1 %reduce-scatter.5.cloned.1.call-start = ((), (), s32[]{:S(2)}) async-start(), calls=%async_computation.4 | async-start | bytes 2162688 | tf_op jit(solution)/shard_map/reduce_scatter | solution.py:49
  34.9 48.7 %copy-start.4 = (s32[128,128]{1,0:T(8,128)S(1)}, s32[128,128]{1,0:T(8,128)}, u32[]{:S(2)}) copy-start(s32[128,128]{1,0:T(8,128)} %param.6) | copy-start | bytes 196612
  34.9 94.8 %copy-start.2 = (s32[128,128]{1,0:T(8,128)S(1)}, s32[128,128]{1,0:T(8,128)}, u32[]{:S(2)}) copy-start(s32[128,128]{1,0:T(8,128)} %param.7) | copy-start | bytes 196612
  135.4 1.9 copy-start.1
  137.3 1.9 copy-start.5
  137.3 109.8 %copy-start.3 = (bf16[128,128]{1,0:T(8,128)(2,1)S(1)}, bf16[128,128]{1,0:T(8,128)(2,1)}, u32[]{:S(2)}) copy-start(bf16[128,128]{1,0:T(8,128)(2,1)} %param.8) | copy-start | bytes 98308
  137.3 202.0 %reduce-scatter.3.cloned.1.call-start = ((), (), s32[]{:S(2)}) async-start(), calls=%async_computation.3 | async-start | bytes 2228224 | tf_op jit(solution)/shard_map/reduce_scatter | solution.py:43
Sparse Core Ops, SparseCore 0:
  11.1 63.9 all-gather.2
  137.4 109.6 reduce-scatter.4
  249.9 63.9 reduce-scatter.2
where the time goes:
time: 352 us; the launch traced here: 347 us
  blocking collectives  159 us (45%)
  waiting for transfers between devices  149 us (42%)
  other arithmetic  19.6 us (6%)
  between operations  13.9 us (4%)
  matrix products  5.36 us (2%)
    reduce_scatter x1, waiting for transfers between devices, shards(): lax.psum_scatter(partial_grads, 'query', scatter_dimension=1, tiled=True)  108 us
    psum x1, blocking collectives, shards(): lax.psum(jnp.sum(scaled * hidden_slice, axis=1), 'query') / float(D)  64.3 us
    all_gather x1, waiting for transfers between devices, shards(): lax.all_gather(hidden_states, 'query', axis=1, tiled=True)  40.2 us
    psum x1, blocking collectives, shards(): lax.psum(jnp.sum(e_slice * hidden_slice * inv_rms[:, None], axis=0), 'pas...  25.4 us
    pmax x1, blocking collectives, shards(): top_score = lax.pmax(jnp.max(masked, axis=1), 'passage')  24.7 us
    all_gather x1, blocking collectives, shards(): lax.all_gather(gain, 'query', axis=0, tiled=True)  24.1 us
    psum x1, blocking collectives, shards(): lax.psum(jnp.sum(jnp.where(is_owned, jnp.exp(masked - top_score[:, None])...  21 us
  transfers between devices with their start and end apart: 3, of which 2 were waited for; matrix products, arithmetic and copies ran while one was open for 2% of the time, Pallas kernels for 0%

commit v1 on v0

v1 whole, which is shorter than its diff:
```python
import jax
import jax.numpy as jnp
from jax import lax
from jax.experimental import pallas as pl
from jax.experimental.pallas import tpu as pltpu
from jax.sharding import PartitionSpec as P

D = 4096
MESH = pl.DeviceIdType.MESH
F32, BF16, I32 = jnp.float32, jnp.bfloat16, jnp.int32
NZ = 16
NC = 16
B = 128
X = 144


def lanes(x, index):
    return jnp.take_along_axis(x, index, axis=1)


def kernel(
    q_ref, cand_ref, teach_ref, hid_ref, gain_ref,
    qg_ref, hg_ref, gg_ref,
    hf, hid32, xp, xz, ez, emb, inv, invp, tgt, tgt_t, sg, stat_s, stat_r, sp_s, sp_r,
    lg_s, lg_r, gfull, embz, eb, e32, sib_r, gs, gsib_r, gm_s, gm_r, s6_s, s6_r, z7_s, z7_r,
    s1_sem, s1_dir, s1_rel, small_sem, xz_sem, st_sem, sp_sem, lg_sem, ez_sem, ez_dir, ez_rel,
    sib_sem, gsib_sem, gm_sem, s6_sem, z7_sem,
):
    me = lax.axis_index("query")
    z = lax.axis_index("passage")
    core = lax.bitwise_and(me, 1)
    other = 1 - core
    chip = lax.shift_right_logical(me, 1)
    cy, cx = lax.shift_right_logical(chip, 2), lax.bitwise_and(chip, 3)
    sibling = {"query": 2 * chip + other}

    def chip_at(d):
        ty = lax.bitwise_and(cy + lax.shift_right_logical(d, 2), 3)
        tx = lax.bitwise_and(cx + d, 3)
        return 4 * ty + tx

    def z_at(d):
        return lax.bitwise_and(z + d, NZ - 1)

    def each(first, last, body):
        def step(d, carry):
            body(d)
            return carry

        lax.fori_loop(first, last, step, 0)

    def send(src, dst, s_sem, r_sem, where):
        pltpu.make_async_remote_copy(
            src_ref=src, dst_ref=dst, send_sem=s_sem, recv_sem=r_sem,
            device_id=where, device_id_type=MESH,
        ).start()

    def drain(ref, sem):
        pltpu.make_async_copy(ref, ref, sem).wait()

    barrier = pltpu.get_barrier_semaphore()

    def hail_z(d):
        pl.semaphore_signal(barrier, inc=1, device_id={"passage": z_at(d)}, device_id_type=MESH)

    def hail_plane(d):
        pl.semaphore_signal(
            barrier, inc=1, device_id={"query": lax.bitwise_and(me + d, 31)}, device_id_type=MESH
        )

    each(1, NZ, hail_z)
    each(1, 32, hail_plane)

    hid = hid_ref[...]
    gain_row = gain_ref[...].astype(F32)
    hf[core, chip, 0:B, :] = hid
    hf[core, chip, B:X, :] = jnp.broadcast_to(gain_row, (16, B)).astype(BF16)
    h32 = hid.astype(F32)
    hid32[...] = h32.reshape(NC, 8, B)
    xp[chip] = hid32[chip]

    t = teach_ref[...].astype(F32) * 0.125
    t = jnp.exp(t - jnp.max(t, axis=1, keepdims=True))
    tgt[...] = t / jnp.sum(t, axis=1, keepdims=True)

    lane = lax.broadcasted_iota(I32, (8, B), 1)
    owned_id = lane + z * B
    base = lax.shift_left(lax.shift_right_logical(lane, 3), 7) + lax.bitwise_and(lane, 7)

    def own_inverse(g):
        rows = pl.ds(pl.multiple_of(g * 8, 8), 8)
        cand = cand_ref[rows, :]
        acc = jnp.full((8, B), -1, I32)
        for c in range(B):
            acc = jnp.where(cand[:, c : c + 1] == owned_id, c, acc)
        invp[rows, :] = acc

    def full_inverse(g):
        rows = pl.ds(pl.multiple_of(g * 8, 8), 8)
        cand = cand_ref[rows, :]
        accs = [jnp.full((8, B), -1, I32) for _ in range(NC)]
        for c in range(B):
            one = jnp.broadcast_to(cand[:, c : c + 1], (8, B))
            for b in range(NC):
                accs[b] = jnp.where(one == base + 8 * b, c, accs[b])
        for b in range(NC):
            inv[rows, b * B : (b + 1) * B] = accs[b]

    each(0, 16, own_inverse)
    each(0, 8, full_inverse)

    pl.semaphore_wait(barrier, NZ - 1 + 31)

    def send_small(d):
        t = chip_at(d)
        send(hid32.at[t], xp.at[chip], small_sem.at[0], small_sem.at[1], {"query": 2 * t + core})

    def send_hidden(d):
        t = chip_at(d)
        block = hf.at[core, chip]
        send(block, block, s1_sem.at[0], s1_dir.at[chip], {"query": 2 * t + core})

    each(1, NC, send_small)
    own = hf.at[core, chip]
    send(own, own, s1_sem.at[1], s1_rel.at[0], sibling)
    each(1, NC, send_hidden)

    each(8, 16, full_inverse)

    drain(xp.at[pl.ds(0, NC - 1)], small_sem.at[1])
    xz[z] = xp[z]

    def send_slice(d):
        t = z_at(d)
        send(xp.at[t], xz.at[z], xz_sem.at[0], xz_sem.at[1], {"passage": t})

    each(1, NZ, send_slice)

    def relay_hidden(d):
        f = 4 * lax.bitwise_and(cy - lax.shift_right_logical(d, 2) + 4, 3) + lax.bitwise_and(cx - d + NC, 3)
        block = hf.at[core, f]
        drain(block, s1_dir.at[f])
        send(block, block, s1_sem.at[1], s1_rel.at[0], sibling)

    each(1, NC, relay_hidden)
    drain(hf.at[other], s1_rel.at[0])

    total = jnp.zeros((B, B), F32)
    for c in range(NC):
        for k in range(2):
            x = hf[k, c, 0:B, :].astype(F32)
            total = total + x * x
    inv_rms = lax.rsqrt(jnp.sum(total, axis=1, keepdims=True) / float(D) + 1e-05)
    for c in range(NC):
        for k in range(2):
            x = hf[k, c, 0:B, :].astype(F32)
            g = hf[k, c, B:X, :].astype(F32)[0:1, :]
            emb[:, (2 * c + k) * B : (2 * c + k + 1) * B] = (x * inv_rms * g).astype(BF16)
    scale = float(D) ** -0.5
    scores_t = (
        lax.dot_general(emb[...], q_ref[...], (((1,), (1,)), ((), ())), preferred_element_type=F32) * scale
    )
    inv_own = invp[...]
    listed = inv_own >= 0
    listed_t = listed.astype(F32).T > 0.0
    masked = jnp.where(listed_t, scores_t, -1e30)
    top = jnp.max(masked, axis=0, keepdims=True)
    weight = jnp.where(listed_t, jnp.exp(masked - top), 0.0)
    part = jnp.sum(weight, axis=0, keepdims=True)
    stat_s[0:1, :] = top
    stat_s[1:2, :] = part
    stat_r[z] = stat_s[...]

    def send_stat(d):
        send(stat_s, stat_r.at[z], st_sem.at[0], st_sem.at[1], {"passage": z_at(d)})

    each(1, NZ, send_stat)

    scores = scores_t.T
    for g in range(16):
        rows = slice(8 * g, 8 * g + 8)
        local = cand_ref[rows, :] - z * B
        mine = (local >= 0) & (local < B)
        sp_s[g] = jnp.where(mine, lanes(scores[rows, :], jnp.clip(local, 0, B - 1)), 0.0)
    sp_r[z] = sp_s[z]

    def send_sparse(d):
        t = z_at(d)
        send(sp_s.at[t], sp_r.at[z], sp_sem.at[0], sp_sem.at[1], {"passage": t})

    each(1, NZ, send_sparse)

    drain(xz.at[pl.ds(0, NZ - 1)], xz_sem.at[1])
    ez[core, chip] = xz[...].reshape(B, B).astype(BF16)

    def send_rows(d):
        t = chip_at(d)
        block = ez.at[core, chip]
        send(block, block, ez_sem.at[0], ez_dir.at[chip], {"query": 2 * t + core})

    own_rows = ez.at[core, chip]
    send(own_rows, own_rows, ez_sem.at[1], ez_rel.at[0], sibling)
    each(1, NC, send_rows)

    for g in range(16):
        rows = slice(8 * g, 8 * g + 8)
        i = inv_own[rows, :]
        sg[rows, :] = jnp.where(i >= 0, lanes(tgt[rows, :], jnp.maximum(i, 0)), 0.0)
    tgt_t[...] = sg[...].T

    drain(stat_r.at[pl.ds(0, NZ - 1)], st_sem.at[1])
    tops = [stat_r[k, 0:1, :] for k in range(NZ)]
    parts = [stat_r[k, 1:2, :] for k in range(NZ)]
    top_all = tops[0]
    for k in range(1, NZ):
        top_all = jnp.maximum(top_all, tops[k])
    norm = jnp.zeros((1, B), F32)
    for k in range(NZ):
        norm = norm + parts[k] * jnp.exp(tops[k] - top_all)
    table_t = jnp.where(listed_t, jnp.exp(masked - top_all) / norm - tgt_t[...], 0.0).astype(BF16)
    row_dot = jnp.sum(table_t.astype(F32) * scores_t, axis=1, keepdims=True)
    row_dot_row = jnp.broadcast_to(row_dot, (B, B)).T[0:1, :]
    for c in range(NC):
        both = jnp.dot(table_t, q_ref[:, c * 256 : (c + 1) * 256], preferred_element_type=F32)
        for k in range(2):
            e = both[:, k * B : (k + 1) * B]
            e32[k, c] = e
            eb[k, c] = e.astype(BF16)
            terms = e * hf[k, c, 0:B, :].astype(F32) * inv_rms
            gs[k, c, 0:1, :] = jnp.sum(terms, axis=0, keepdims=True)
            gs[k, c, 1:2, :] = row_dot_row
    send(gs.at[other], gsib_r, gsib_sem.at[0], gsib_sem.at[1], sibling)
    send(eb.at[other], sib_r, sib_sem.at[0], sib_sem.at[1], sibling)

    drain(sp_r.at[pl.ds(0, NZ - 1)], sp_sem.at[1])
    logits = sp_r[0]
    for k in range(1, NZ):
        logits = logits + sp_r[k]
    w = jnp.exp(logits - jnp.max(logits, axis=1, keepdims=True))
    student = w / jnp.sum(w, axis=1, keepdims=True)
    my_rows = pl.ds(pl.multiple_of(z * 8, 8), 8)
    lg_s[0:8, :] = (student - tgt[my_rows, :]).astype(BF16).astype(F32)
    lg_s[8:16, :] = jnp.broadcast_to(inv_rms, (B, B)).T[0:8, :]
    lg_r[z] = lg_s[...]

    def send_list(d):
        send(lg_s, lg_r.at[z], lg_sem.at[0], lg_sem.at[1], {"passage": z_at(d)})

    each(1, NZ, send_list)

    drain(gsib_r, gsib_sem.at[1])
    for c in range(NC):
        gm_s[c] = gs[core, c] + gsib_r[c]
    gm_r[chip] = gm_s[chip]

    def send_gain(d):
        t = chip_at(d)
        send(gm_s.at[t], gm_r.at[chip], gm_sem.at[0], gm_sem.at[1], {"query": 2 * t + core})

    each(1, NC, send_gain)
    drain(sib_r, sib_sem.at[1])
    for c in range(NC):
        s6_s[c] = (e32[core, c] + sib_r[c].astype(F32)).astype(BF16)
    s6_r[chip] = s6_s[chip]

    def send_grads(d):
        t = chip_at(d)
        send(s6_s.at[t], s6_r.at[chip], s6_sem.at[0], s6_sem.at[1], {"query": 2 * t + core})

    each(1, NC, send_grads)

    def relay_rows(d):
        f = 4 * lax.bitwise_and(cy - lax.shift_right_logical(d, 2) + 4, 3) + lax.bitwise_and(cx - d + NC, 3)
        block = ez.at[core, f]
        drain(block, ez_dir.at[f])
        send(block, block, ez_sem.at[1], ez_rel.at[0], sibling)

    each(1, NC, relay_rows)

    drain(gm_r.at[pl.ds(0, NC - 1)], gm_sem.at[1])
    small = gm_r[0]
    for c in range(1, NC):
        small = small + gm_r[c]
    z7_s[...] = small
    z7_r[z] = small

    def send_plane_gain(d):
        send(z7_s, z7_r.at[z], z7_sem.at[0], z7_sem.at[1], {"passage": z_at(d)})

    each(1, NZ, send_plane_gain)

    drain(lg_r.at[pl.ds(0, NZ - 1)], lg_sem.at[1])
    for g in range(0, 16, 2):
        for b in range(NC):
            cols = slice(b * B, (b + 1) * B)
            two = []
            for k in (g, g + 1):
                i = inv[8 * k : 8 * k + 8, cols]
                two.append(jnp.where(i >= 0, lanes(lg_r[k, 0:8, :], jnp.maximum(i, 0)), 0.0))
            gfull[8 * g : 8 * g + 16, cols] = jnp.concatenate(two, axis=0).astype(BF16)
    drain(ez.at[other], ez_rel.at[0])
    rms_rows = jnp.concatenate([lg_r[k, 8:9, :] for k in range(NZ)], axis=0)
    rms_t = jnp.concatenate([rms_rows, jnp.zeros((B - NZ, B), F32)], axis=0).T
    gains = [hf[k, z, B:X, :].astype(F32)[0:1, :] for k in range(2)]
    for c in range(NC):
        col = jnp.concatenate(
            [jnp.broadcast_to(rms_t[8 * c : 8 * c + 8, k : k + 1], (8, B)) for k in range(NZ)], axis=0
        )
        for k in range(2):
            raw = ez[k, c].astype(F32)
            embz[c * B : (c + 1) * B, k * B : (k + 1) * B] = (raw * col * gains[k]).astype(BF16)
    qg_ref[...] = jnp.dot(gfull[...], embz[...], preferred_element_type=F32).astype(BF16)

    drain(s6_r.at[pl.ds(0, NC - 1)], s6_sem.at[1])
    e_grad = s6_r[0].astype(F32)
    for c in range(1, NC):
        e_grad = e_grad + s6_r[c].astype(F32)
    dot_col = jnp.broadcast_to(small[1:2, :], (B, B)).T
    hg_ref[...] = (
        inv_rms * (e_grad * gain_row) - hid_ref[...].astype(F32) * (inv_rms * inv_rms) * (dot_col * scale)
    ).astype(BF16)

    drain(z7_r.at[pl.ds(0, NZ - 1)], z7_sem.at[1])
    gain_grad = z7_r[0, 0:1, :]
    for k in range(1, NZ):
        gain_grad = gain_grad + z7_r[k, 0:1, :]
    gg_ref[...] = gain_grad

    n = NC - 1
    drain(xp.at[pl.ds(0, n)], small_sem.at[0])
    drain(hf.at[0, pl.ds(0, n)], s1_sem.at[0])
    drain(hf.at[0], s1_sem.at[1])
    drain(xz.at[pl.ds(0, n)], xz_sem.at[0])
    drain(stat_r.at[pl.ds(0, n)], st_sem.at[0])
    drain(sp_r.at[pl.ds(0, n)], sp_sem.at[0])
    drain(lg_r.at[pl.ds(0, n)], lg_sem.at[0])
    drain(ez.at[0, pl.ds(0, n)], ez_sem.at[0])
    drain(ez.at[0], ez_sem.at[1])
    drain(gsib_r, gsib_sem.at[0])
    drain(sib_r, sib_sem.at[0])
    drain(gm_r.at[pl.ds(0, n)], gm_sem.at[0])
    drain(s6_r.at[pl.ds(0, n)], s6_sem.at[0])
    drain(z7_r.at[pl.ds(0, n)], z7_sem.at[0])


def shards(queries, cand_ids, teacher, hidden_states, gain):
    vmem = pl.BlockSpec(memory_space=pltpu.VMEM)
    two = pltpu.SemaphoreType.DMA((2,))
    q_grad, h_grad, gain_grad = pl.pallas_call(
        kernel,
        name="listwise",
        out_shape=(
            jax.ShapeDtypeStruct((B, 2 * B), BF16),
            jax.ShapeDtypeStruct((B, B), BF16),
            jax.ShapeDtypeStruct((1, B), F32),
        ),
        in_specs=[vmem] * 5,
        out_specs=(vmem, vmem, vmem),
        scratch_shapes=[
            pltpu.VMEM((2, NC, X, B), BF16),
            pltpu.VMEM((NC, 8, B), F32),
            pltpu.VMEM((NC, 8, B), F32),
            pltpu.VMEM((NZ, 8, B), F32),
            pltpu.VMEM((2, NC, B, B), BF16),
            pltpu.VMEM((B, D), BF16),
            pltpu.VMEM((B, NC * B), I32),
            pltpu.VMEM((B, B), I32),
            pltpu.VMEM((B, B), F32),
            pltpu.VMEM((B, B), F32),
            pltpu.VMEM((B, B), F32),
            pltpu.VMEM((8, B), F32),
            pltpu.VMEM((NZ, 8, B), F32),
            pltpu.VMEM((NZ, 8, B), F32),
            pltpu.VMEM((NZ, 8, B), F32),
            pltpu.VMEM((16, B), F32),
            pltpu.VMEM((NZ, 16, B), F32),
            pltpu.VMEM((B, NC * B), BF16),
            pltpu.VMEM((NC * B, 2 * B), BF16),
            pltpu.VMEM((2, NC, B, B), BF16),
            pltpu.VMEM((2, NC, B, B), F32),
            pltpu.VMEM((NC, B, B), BF16),
            pltpu.VMEM((2, NC, 8, B), F32),
            pltpu.VMEM((NC, 8, B), F32),
            pltpu.VMEM((NC, 8, B), F32),
            pltpu.VMEM((NC, 8, B), F32),
            pltpu.VMEM((NC, B, B), BF16),
            pltpu.VMEM((NC, B, B), BF16),
            pltpu.VMEM((8, B), F32),
            pltpu.VMEM((NZ, 8, B), F32),
            two,
            pltpu.SemaphoreType.DMA((NC,)),
            pltpu.SemaphoreType.DMA((1,)),
            two,
            two,
            two,
            two,
            two,
            two,
            pltpu.SemaphoreType.DMA((NC,)),
            pltpu.SemaphoreType.DMA((1,)),
            two,
            two,
            two,
            two,
            two,
        ],
        compiler_params=pltpu.CompilerParams(
            collective_id=0, has_side_effects=True, vmem_limit_bytes=48 * 2**20
        ),
    )(queries, cand_ids, teacher, hidden_states, gain.reshape(1, B))
    return q_grad, h_grad, gain_grad.reshape(B)


def solution(mesh):
    placed = (
        P("query", None),
        P("query", None),
        P("query", None),
        P("passage", "query"),
        P("query"),
    )
    return jax.shard_map(
        shards,
        mesh=mesh,
        in_specs=placed,
        out_specs=(P("query", "passage"), P("passage", "query"), P("query")),
        check_vma=False,
    )
```

time: 352 us -> 64.8 us (0.18); the launches traced: 347 us -> 64.4 us
  blocking collectives: 159 us -> 0 us
  waiting for transfers between devices: 149 us -> 0 us
  Pallas kernels: 0 us -> 57.7 us
  other arithmetic: 19.6 us -> 0 us
  between operations: 13.9 us -> 0.65 us
  local copies, waits for them, and re-layouts: 0.12 us -> 6.07 us
  matrix products: 5.36 us -> 0 us
    psum x3 -> x0, blocking collectives: 111 us -> none  [the longest x1 64.3 us: shards(): lax.psum(jnp.sum(scaled * hidden_slice, axis=1), 'query') / float(D)]
    reduce_scatter x2 -> x0, waiting for transfers between devices: 108 us -> none  [the longest x1 108 us: shards(): lax.psum_scatter(partial_grads, 'query', scatter_dimension=1, tiled=True)]
    pallas_call x0 -> x1, Pallas kernels: none -> 57.7 us  [shards(): pl.pallas_call(kernel, name='listwise', out_shape=(jax.ShapeDtypeStruct((...]
    all_gather x1 -> x0, waiting for transfers between devices: 40.2 us -> none  [shards(): lax.all_gather(hidden_states, 'query', axis=1, tiled=True)]
    pmax x1 -> x0, blocking collectives: 24.7 us -> none  [shards(): top_score = lax.pmax(jnp.max(masked, axis=1), 'passage')]
    all_gather x1 -> x0, blocking collectives: 24.1 us -> none  [shards(): lax.all_gather(gain, 'query', axis=0, tiled=True)]
    reduce_sum x6 -> x0, other arithmetic: 14.4 us -> none  [the longest x1 5.61 us: shards(): jnp.sum(jnp.where(matches, list_grad[:, :, None], 0.0), axis=1)]
    unnamed x12 -> x13, local copies, waits for them, and re-layouts: 0.03 us -> 6.07 us
  transfers between devices with their start and end apart: 3 -> 0, of which waited for: 2 -> 0; matrix products, arithmetic and copies ran while one was open for 2% -> 0% of each run, Pallas kernels for 0% -> 0%
where the time goes in v1:
time: 64.8 us; the launch traced here: 64.4 us
  Pallas kernels  57.7 us (89%)
  local copies, waits for them, and re-layouts  6.07 us (9%)
  between operations  0.65 us (1%)
    pallas_call x1, Pallas kernels, shards(): pl.pallas_call(kernel, name='listwise', out_shape=(jax.ShapeDtypeStruct((...  57.7 us
    unnamed x13, local copies, waits for them, and re-layouts  6.07 us

profile of v1, /device:TPU:1, one launch (start us, length us, event | category | flops | bytes accessed | tf_op | source)
XLA Modules:
  0.0 64.4 jit_solution(15288811721317568588)
XLA Ops:
  0.6 0.0 copy-start.4
  0.6 0.6 %copy-done.4 = bf16[128]{0:T(256)(128)(2,1)S(1)} copy-done((bf16[128]{0:T(256)(128)(2,1)S(1)}, bf16[128]{0:T(256)(128)(2,1)}, u32[]{:S(2)}) %copy-start.4) | copy-done | bytes 280
  1.3 0.0 copy-start
  1.3 1.2 %copy-done = bf16[128,4096]{1,0:T(8,128)(2,1)S(1)} copy-done((bf16[128,4096]{1,0:T(8,128)(2,1)S(1)}, bf16[128,4096]{1,0:T(8,128)(2,1)}, u32[]{:S(2)}) %copy-start) | copy-done | bytes 1048600
  2.5 0.0 copy-start.1
  2.5 0.8 %copy-done.1 = s32[128,128]{1,0:T(8,128)S(1)} copy-done((s32[128,128]{1,0:T(8,128)S(1)}, s32[128,128]{1,0:T(8,128)}, u32[]{:S(2)}) %copy-start.1) | copy-done | bytes 65560
  3.4 0.0 copy-start.2
  3.4 0.8 %copy-done.2 = s32[128,128]{1,0:T(8,128)S(1)} copy-done((s32[128,128]{1,0:T(8,128)S(1)}, s32[128,128]{1,0:T(8,128)}, u32[]{:S(2)}) %copy-start.2) | copy-done | bytes 65560
  4.2 0.0 copy-start.3
  4.2 0.8 %copy-done.3 = bf16[128,128]{1,0:T(8,128)(2,1)S(1)} copy-done((bf16[128,128]{1,0:T(8,128)(2,1)S(1)}, bf16[128,128]{1,0:T(8,128)(2,1)}, u32[]{:S(2)}) %copy-start.3) | copy-done | bytes 32792
  5.0 57.7 %listwise.1 = (bf16[128,256]{1,0:T(8,128)(2,1)S(1)}, bf16[128,128]{1,0:T(8,128)(2,1)S(1)}, f32[1,128]{1,0:T(1,128)S(1)}) custom-call(bf16[128,4096]{1,0:T(8,128)(2,1)S(1)} %copy-done, s32[128,128]{1,0:T(8,128)S(1)} %copy-done.1, s32[128,128]{1,0:T(8,128)S(1)} %copy-done.2, bf16[128,128]{1,0:T(8,128)(2,1)S(1)} %copy-done.3, bf16[1,128]{1,0:T(2,128)(2,1)S(1)} %bitcast.2), custom_call_target="tpu_custom_call" | custom-call | tf_op jit(solution)/shard_map/listwise/pallas_call | solution.py:349
  62.6 0.6 copy.11
  63.3 0.6 copy.12
  63.9 0.5 copy.13
Async XLA Ops:
  0.6 0.7 %copy-start.4 = (bf16[128]{0:T(256)(128)(2,1)S(1)}, bf16[128]{0:T(256)(128)(2,1)}, u32[]{:S(2)}) copy-start(bf16[128]{0:T(256)(128)(2,1)} %param.9) | copy-start | bytes 772
  1.3 1.2 %copy-start = (bf16[128,4096]{1,0:T(8,128)(2,1)S(1)}, bf16[128,4096]{1,0:T(8,128)(2,1)}, u32[]{:S(2)}) copy-start(bf16[128,4096]{1,0:T(8,128)(2,1)} %q_ref.1) | copy-start | bytes 3145732
  2.5 0.8 %copy-start.1 = (s32[128,128]{1,0:T(8,128)S(1)}, s32[128,128]{1,0:T(8,128)}, u32[]{:S(2)}) copy-start(s32[128,128]{1,0:T(8,128)} %cand_ref.1) | copy-start | bytes 196612
  3.4 0.8 %copy-start.2 = (s32[128,128]{1,0:T(8,128)S(1)}, s32[128,128]{1,0:T(8,128)}, u32[]{:S(2)}) copy-start(s32[128,128]{1,0:T(8,128)} %teach_ref.1) | copy-start | bytes 196612
  4.2 0.8 %copy-start.3 = (bf16[128,128]{1,0:T(8,128)(2,1)S(1)}, bf16[128,128]{1,0:T(8,128)(2,1)}, u32[]{:S(2)}) copy-start(bf16[128,128]{1,0:T(8,128)(2,1)} %hid_ref.1) | copy-start | bytes 98308

commit v2 on v1

--- a/solution.py
+++ b/solution.py
@@ -8,6 +8,8 @@
 D = 4096
 MESH = pl.DeviceIdType.MESH
 F32, BF16, I32 = jnp.float32, jnp.bfloat16, jnp.int32
+FAR_FIRST = (10, 6, 9, 11, 14, 2, 8, 5, 7, 13, 15, 1, 3, 4, 12)
+FAR_Z = (8, 7, 9, 6, 10, 5, 11, 4, 12, 3, 13, 2, 14, 1, 15)
 NZ = 16
 NC = 16
 B = 128
@@ -19,12 +21,13 @@
 
 
 def kernel(
-    q_ref, cand_ref, teach_ref, hid_ref, gain_ref,
+    q_hbm, cand_hbm, teach_hbm, hid_hbm, gain_hbm,
     qg_ref, hg_ref, gg_ref,
+    q_ref, cand_ref, teach_ref, hid_ref, gain_ref, in_sem,
     hf, hid32, xp, xz, ez, emb, inv, invp, tgt, tgt_t, sg, stat_s, stat_r, sp_s, sp_r,
-    lg_s, lg_r, gfull, embz, eb, e32, sib_r, gs, gsib_r, gm_s, gm_r, s6_s, s6_r, z7_s, z7_r,
+    lg_s, lg_r, gfull, embz, eb, e32, sib_r, gs, gm_r, s6_s, s6_r, z7_s, z7_r,
     s1_sem, s1_dir, s1_rel, small_sem, xz_sem, st_sem, sp_sem, lg_sem, ez_sem, ez_dir, ez_rel,
-    sib_sem, gsib_sem, gm_sem, s6_sem, z7_sem,
+    sib_sem, gm_sem, s6_sem, z7_sem,
 ):
     me = lax.axis_index("query")
     z = lax.axis_index("passage")
@@ -35,12 +38,23 @@
     sibling = {"query": 2 * chip + other}
 
     def chip_at(d):
-        ty = lax.bitwise_and(cy + lax.shift_right_logical(d, 2), 3)
+        ty = lax.bitwise_and(cy + d // 4, 3)
         tx = lax.bitwise_and(cx + d, 3)
         return 4 * ty + tx
 
+    def chip_from(d):
+        return 4 * lax.bitwise_and(cy - d // 4 + 4, 3) + lax.bitwise_and(cx - d + NC, 3)
+
     def z_at(d):
         return lax.bitwise_and(z + d, NZ - 1)
+
+    def plane_loop(body):
+        for d in FAR_FIRST:
+            body(d)
+
+    def z_loop(body):
+        for d in FAR_Z:
+            body(d)
 
     def each(first, last, body):
         def step(d, carry):
@@ -58,6 +72,15 @@
     def drain(ref, sem):
         pltpu.make_async_copy(ref, ref, sem).wait()
 
+    arguments = [
+        pltpu.make_async_copy(src, dst, in_sem.at[k])
+        for k, (src, dst) in enumerate(
+            [(hid_hbm, hid_ref), (gain_hbm, gain_ref), (cand_hbm, cand_ref), (teach_hbm, teach_ref), (q_hbm, q_ref)]
+        )
+    ]
+    for argument in arguments:
+        argument.start()
+
     barrier = pltpu.get_barrier_semaphore()
 
     def hail_z(d):
@@ -68,9 +91,11 @@
             barrier, inc=1, device_id={"query": lax.bitwise_and(me + d, 31)}, device_id_type=MESH
         )
 
-    each(1, NZ, hail_z)
+    z_loop(hail_z)
     each(1, 32, hail_plane)
 
+    arguments[0].wait()
+    arguments[1].wait()
     hid = hid_ref[...]
     gain_row = gain_ref[...].astype(F32)
     hf[core, chip, 0:B, :] = hid
@@ -79,6 +104,8 @@
     hid32[...] = h32.reshape(NC, 8, B)
     xp[chip] = hid32[chip]
 
+    arguments[2].wait()
+    arguments[3].wait()
     t = teach_ref[...].astype(F32) * 0.125
     t = jnp.exp(t - jnp.max(t, axis=1, keepdims=True))
     tgt[...] = t / jnp.sum(t, axis=1, keepdims=True)
@@ -88,12 +115,14 @@
     base = lax.shift_left(lax.shift_right_logical(lane, 3), 7) + lax.bitwise_and(lane, 7)
 
     def own_inverse(g):
-        rows = pl.ds(pl.multiple_of(g * 8, 8), 8)
-        cand = cand_ref[rows, :]
-        acc = jnp.full((8, B), -1, I32)
+        rows = [pl.ds(pl.multiple_of(g * 32 + 8 * k, 8), 8) for k in range(4)]
+        cands = [cand_ref[r, :] for r in rows]
+        accs = [jnp.full((8, B), -1, I32) for _ in rows]
         for c in range(B):
-            acc = jnp.where(cand[:, c : c + 1] == owned_id, c, acc)
-        invp[rows, :] = acc
+            for k in range(4):
+                accs[k] = jnp.where(cands[k][:, c : c + 1] == owned_id, c, accs[k])
+        for k in range(4):
+            invp[rows[k], :] = accs[k]
 
     def full_inverse(g):
         rows = pl.ds(pl.multiple_of(g * 8, 8), 8)
@@ -106,8 +135,7 @@
         for b in range(NC):
             inv[rows, b * B : (b + 1) * B] = accs[b]
 
-    each(0, 16, own_inverse)
-    each(0, 8, full_inverse)
+    each(0, 4, own_inverse)
 
     pl.semaphore_wait(barrier, NZ - 1 + 31)
 
@@ -120,12 +148,12 @@
         block = hf.at[core, chip]
         send(block, block, s1_sem.at[0], s1_dir.at[chip], {"query": 2 * t + core})
 
-    each(1, NC, send_small)
+    plane_loop(send_small)
     own = hf.at[core, chip]
     send(own, own, s1_sem.at[1], s1_rel.at[0], sibling)
-    each(1, NC, send_hidden)
-
-    each(8, 16, full_inverse)
+    plane_loop(send_hidden)
+
+    each(0, 4, full_inverse)
 
     drain(xp.at[pl.ds(0, NC - 1)], small_sem.at[1])
     xz[z] = xp[z]
@@ -134,15 +162,15 @@
         t = z_at(d)
         send(xp.at[t], xz.at[z], xz_sem.at[0], xz_sem.at[1], {"passage": t})
 
-    each(1, NZ, send_slice)
+    z_loop(send_slice)
 
     def relay_hidden(d):
-        f = 4 * lax.bitwise_and(cy - lax.shift_right_logical(d, 2) + 4, 3) + lax.bitwise_and(cx - d + NC, 3)
+        f = chip_from(d)
         block = hf.at[core, f]
         drain(block, s1_dir.at[f])
         send(block, block, s1_sem.at[1], s1_rel.at[0], sibling)
 
-    each(1, NC, relay_hidden)
+    plane_loop(relay_hidden)
     drain(hf.at[other], s1_rel.at[0])
 
     total = jnp.zeros((B, B), F32)
@@ -156,7 +184,9 @@
             x = hf[k, c, 0:B, :].astype(F32)
             g = hf[k, c, B:X, :].astype(F32)[0:1, :]
             emb[:, (2 * c + k) * B : (2 * c + k + 1) * B] = (x * inv_rms * g).astype(BF16)
+    rms_row = jnp.broadcast_to(inv_rms, (B, B)).T[0:1, :]
     scale = float(D) ** -0.5
+    arguments[4].wait()
     scores_t = (
         lax.dot_general(emb[...], q_ref[...], (((1,), (1,)), ((), ())), preferred_element_type=F32) * scale
     )
@@ -169,12 +199,13 @@
     part = jnp.sum(weight, axis=0, keepdims=True)
     stat_s[0:1, :] = top
     stat_s[1:2, :] = part
+    stat_s[2:3, :] = rms_row
     stat_r[z] = stat_s[...]
 
     def send_stat(d):
         send(stat_s, stat_r.at[z], st_sem.at[0], st_sem.at[1], {"passage": z_at(d)})
 
-    each(1, NZ, send_stat)
+    z_loop(send_stat)
 
     scores = scores_t.T
     for g in range(16):
@@ -188,7 +219,7 @@
         t = z_at(d)
         send(sp_s.at[t], sp_r.at[z], sp_sem.at[0], sp_sem.at[1], {"passage": t})
 
-    each(1, NZ, send_sparse)
+    z_loop(send_sparse)
 
     drain(xz.at[pl.ds(0, NZ - 1)], xz_sem.at[1])
     ez[core, chip] = xz[...].reshape(B, B).astype(BF16)
@@ -200,13 +231,15 @@
 
     own_rows = ez.at[core, chip]
     send(own_rows, own_rows, ez_sem.at[1], ez_rel.at[0], sibling)
-    each(1, NC, send_rows)
+    plane_loop(send_rows)
 
     for g in range(16):
         rows = slice(8 * g, 8 * g + 8)
         i = inv_own[rows, :]
         sg[rows, :] = jnp.where(i >= 0, lanes(tgt[rows, :], jnp.maximum(i, 0)), 0.0)
     tgt_t[...] = sg[...].T
+
+    each(4, 12, full_inverse)
 
     drain(stat_r.at[pl.ds(0, NZ - 1)], st_sem.at[1])
     tops = [stat_r[k, 0:1, :] for k in range(NZ)]
@@ -227,9 +260,17 @@
             e32[k, c] = e
             eb[k, c] = e.astype(BF16)
             terms = e * hf[k, c, 0:B, :].astype(F32) * inv_rms
-            gs[k, c, 0:1, :] = jnp.sum(terms, axis=0, keepdims=True)
-            gs[k, c, 1:2, :] = row_dot_row
-    send(gs.at[other], gsib_r, gsib_sem.at[0], gsib_sem.at[1], sibling)
+            gs[2 * c + k, 0:1, :] = jnp.sum(terms, axis=0, keepdims=True)
+            gs[2 * c + k, 1:2, :] = row_dot_row
+    gm_r[me] = gs[me]
+
+    def send_gain(d):
+        for k in (core, other):
+            t = 2 * chip_at(d) + k
+            send(gs.at[t], gm_r.at[me], gm_sem.at[0], gm_sem.at[1], {"query": t})
+
+    plane_loop(send_gain)
+    send(gs.at[2 * chip + other], gm_r.at[me], gm_sem.at[0], gm_sem.at[1], sibling)
     send(eb.at[other], sib_r, sib_sem.at[0], sib_sem.at[1], sibling)
 
     drain(sp_r.at[pl.ds(0, NZ - 1)], sp_sem.at[1])
@@ -239,25 +280,14 @@
     w = jnp.exp(logits - jnp.max(logits, axis=1, keepdims=True))
     student = w / jnp.sum(w, axis=1, keepdims=True)
     my_rows = pl.ds(pl.multiple_of(z * 8, 8), 8)
-    lg_s[0:8, :] = (student - tgt[my_rows, :]).astype(BF16).astype(F32)
-    lg_s[8:16, :] = jnp.broadcast_to(inv_rms, (B, B)).T[0:8, :]
+    lg_s[...] = (student - tgt[my_rows, :]).astype(BF16).astype(F32)
     lg_r[z] = lg_s[...]
 
     def send_list(d):
         send(lg_s, lg_r.at[z], lg_sem.at[0], lg_sem.at[1], {"passage": z_at(d)})
 
-    each(1, NZ, send_list)
-
-    drain(gsib_r, gsib_sem.at[1])
-    for c in range(NC):
-        gm_s[c] = gs[core, c] + gsib_r[c]
-    gm_r[chip] = gm_s[chip]
-
-    def send_gain(d):
-        t = chip_at(d)
-        send(gm_s.at[t], gm_r.at[chip], gm_sem.at[0], gm_sem.at[1], {"query": 2 * t + core})
-
-    each(1, NC, send_gain)
+    z_loop(send_list)
+
     drain(sib_r, sib_sem.at[1])
     for c in range(NC):
         s6_s[c] = (e32[core, c] + sib_r[c].astype(F32)).astype(BF16)
@@ -267,39 +297,32 @@
         t = chip_at(d)
         send(s6_s.at[t], s6_r.at[chip], s6_sem.at[0], s6_sem.at[1], {"query": 2 * t + core})
 
-    each(1, NC, send_grads)
+    plane_loop(send_grads)
 
     def relay_rows(d):
-        f = 4 * lax.bitwise_and(cy - lax.shift_right_logical(d, 2) + 4, 3) + lax.bitwise_and(cx - d + NC, 3)
+        f = chip_from(d)
         block = ez.at[core, f]
         drain(block, ez_dir.at[f])
         send(block, block, ez_sem.at[1], ez_rel.at[0], sibling)
 
-    each(1, NC, relay_rows)
-
-    drain(gm_r.at[pl.ds(0, NC - 1)], gm_sem.at[1])
+    plane_loop(relay_rows)
+
+    each(12, 16, full_inverse)
+
+    drain(gm_r.at[pl.ds(0, 31)], gm_sem.at[1])
     small = gm_r[0]
-    for c in range(1, NC):
-        small = small + gm_r[c]
-    z7_s[...] = small
-    z7_r[z] = small
+    for k in range(1, 32):
+        small = small + gm_r[k]
+    z7_s[...] = small[0:1, :]
+    z7_r[z] = small[0:1, :]
 
     def send_plane_gain(d):
         send(z7_s, z7_r.at[z], z7_sem.at[0], z7_sem.at[1], {"passage": z_at(d)})
 
-    each(1, NZ, send_plane_gain)
-
-    drain(lg_r.at[pl.ds(0, NZ - 1)], lg_sem.at[1])
-    for g in range(0, 16, 2):
-        for b in range(NC):
-            cols = slice(b * B, (b + 1) * B)
-            two = []
-            for k in (g, g + 1):
-                i = inv[8 * k : 8 * k + 8, cols]
-                two.append(jnp.where(i >= 0, lanes(lg_r[k, 0:8, :], jnp.maximum(i, 0)), 0.0))
-            gfull[8 * g : 8 * g + 16, cols] = jnp.concatenate(two, axis=0).astype(BF16)
+    z_loop(send_plane_gain)
+
     drain(ez.at[other], ez_rel.at[0])
-    rms_rows = jnp.concatenate([lg_r[k, 8:9, :] for k in range(NZ)], axis=0)
+    rms_rows = jnp.concatenate([stat_r[k, 2:3, :] for k in range(NZ)], axis=0)
     rms_t = jnp.concatenate([rms_rows, jnp.zeros((B - NZ, B), F32)], axis=0).T
     gains = [hf[k, z, B:X, :].astype(F32)[0:1, :] for k in range(2)]
     for c in range(NC):
@@ -309,6 +332,15 @@
         for k in range(2):
             raw = ez[k, c].astype(F32)
             embz[c * B : (c + 1) * B, k * B : (k + 1) * B] = (raw * col * gains[k]).astype(BF16)
+    drain(lg_r.at[pl.ds(0, NZ - 1)], lg_sem.at[1])
+    for g in range(0, 16, 2):
+        for b in range(NC):
+            cols = slice(b * B, (b + 1) * B)
+            two = []
+            for k in (g, g + 1):
+                i = inv[8 * k : 8 * k + 8, cols]
+                two.append(jnp.where(i >= 0, lanes(lg_r[k], jnp.maximum(i, 0)), 0.0))
+            gfull[8 * g : 8 * g + 16, cols] = jnp.concatenate(two, axis=0).astype(BF16)
     qg_ref[...] = jnp.dot(gfull[...], embz[...], preferred_element_type=F32).astype(BF16)
 
     drain(s6_r.at[pl.ds(0, NC - 1)], s6_sem.at[1])
@@ -321,9 +353,9 @@
     ).astype(BF16)
 
     drain(z7_r.at[pl.ds(0, NZ - 1)], z7_sem.at[1])
-    gain_grad = z7_r[0, 0:1, :]
+    gain_grad = z7_r[0]
     for k in range(1, NZ):
-        gain_grad = gain_grad + z7_r[k, 0:1, :]
+        gain_grad = gain_grad + z7_r[k]
     gg_ref[...] = gain_grad
 
     n = NC - 1
@@ -336,9 +368,8 @@
     drain(lg_r.at[pl.ds(0, n)], lg_sem.at[0])
     drain(ez.at[0, pl.ds(0, n)], ez_sem.at[0])
     drain(ez.at[0], ez_sem.at[1])
-    drain(gsib_r, gsib_sem.at[0])
     drain(sib_r, sib_sem.at[0])
-    drain(gm_r.at[pl.ds(0, n)], gm_sem.at[0])
+    drain(gm_r.at[pl.ds(0, 31)], gm_sem.at[0])
     drain(s6_r.at[pl.ds(0, n)], s6_sem.at[0])
     drain(z7_r.at[pl.ds(0, n)], z7_sem.at[0])
 
@@ -346,6 +377,7 @@
 def shards(queries, cand_ids, teacher, hidden_states, gain):
     vmem = pl.BlockSpec(memory_space=pltpu.VMEM)
     two = pltpu.SemaphoreType.DMA((2,))
+    arguments = (queries, cand_ids, teacher, hidden_states, gain.reshape(1, B))
     q_grad, h_grad, gain_grad = pl.pallas_call(
         kernel,
         name="listwise",
@@ -354,9 +386,15 @@
             jax.ShapeDtypeStruct((B, B), BF16),
             jax.ShapeDtypeStruct((1, B), F32),
         ),
-        in_specs=[vmem] * 5,
+        in_specs=[pl.BlockSpec(memory_space=pltpu.HBM)] * 5,
         out_specs=(vmem, vmem, vmem),
         scratch_shapes=[
+            pltpu.VMEM((B, D), BF16),
+            pltpu.VMEM((B, B), I32),
+            pltpu.VMEM((B, B), I32),
+            pltpu.VMEM((B, B), BF16),
+            pltpu.VMEM((1, B), BF16),
+            pltpu.SemaphoreType.DMA((5,)),
             pltpu.VMEM((2, NC, X, B), BF16),
             pltpu.VMEM((NC, 8, B), F32),
             pltpu.VMEM((NC, 8, B), F32),
@@ -368,25 +406,23 @@
             pltpu.VMEM((B, B), F32),
             pltpu.VMEM((B, B), F32),
             pltpu.VMEM((B, B), F32),
+            pltpu.VMEM((4, B), F32),
+            pltpu.VMEM((NZ, 4, B), F32),
+            pltpu.VMEM((NZ, 8, B), F32),
+            pltpu.VMEM((NZ, 8, B), F32),
             pltpu.VMEM((8, B), F32),
             pltpu.VMEM((NZ, 8, B), F32),
-            pltpu.VMEM((NZ, 8, B), F32),
-            pltpu.VMEM((NZ, 8, B), F32),
-            pltpu.VMEM((16, B), F32),
-            pltpu.VMEM((NZ, 16, B), F32),
             pltpu.VMEM((B, NC * B), BF16),
             pltpu.VMEM((NC * B, 2 * B), BF16),
             pltpu.VMEM((2, NC, B, B), BF16),
             pltpu.VMEM((2, NC, B, B), F32),
             pltpu.VMEM((NC, B, B), BF16),
-            pltpu.VMEM((2, NC, 8, B), F32),
-            pltpu.VMEM((NC, 8, B), F32),
-            pltpu.VMEM((NC, 8, B), F32),
-            pltpu.VMEM((NC, 8, B), F32),
+            pltpu.VMEM((32, 2, B), F32),
+            pltpu.VMEM((32, 2, B), F32),
             pltpu.VMEM((NC, B, B), BF16),
             pltpu.VMEM((NC, B, B), BF16),
-            pltpu.VMEM((8, B), F32),
-            pltpu.VMEM((NZ, 8, B), F32),
+            pltpu.VMEM((1, B), F32),
+            pltpu.VMEM((NZ, 1, B), F32),
             two,
             pltpu.SemaphoreType.DMA((NC,)),
             pltpu.SemaphoreType.DMA((1,)),
@@ -398,7 +434,6 @@
             two,
             pltpu.SemaphoreType.DMA((NC,)),
             pltpu.SemaphoreType.DMA((1,)),
-            two,
             two,
             two,
             two,
@@ -407,7 +442,7 @@
         compiler_params=pltpu.CompilerParams(
             collective_id=0, has_side_effects=True, vmem_limit_bytes=48 * 2**20
         ),
-    )(queries, cand_ids, teacher, hidden_states, gain.reshape(1, B))
+    )(*[pltpu.with_memory_space_constraint(x, pltpu.HBM) for x in arguments])
     return q_grad, h_grad, gain_grad.reshape(B)
 
 

time: 64.8 us -> 54.2 us (0.84)
  Pallas kernels: 57.7 us -> 51.5 us
  local copies, waits for them, and re-layouts: 6.07 us -> 1.76 us
    pallas_call x1, Pallas kernels: 57.7 us -> 51.5 us  [shards(): pl.pallas_call(kernel, name='listwise', out_shape=(jax.ShapeDtypeStruct((...]
    unnamed x13 -> x3, local copies, waits for them, and re-layouts: 6.07 us -> 1.76 us
where the time goes in v2:
time: 54.2 us; the launch traced here: 53.9 us
  Pallas kernels  51.5 us (95%)
  local copies, waits for them, and re-layouts  1.76 us (3%)
  between operations  0.64 us (1%)
    pallas_call x1, Pallas kernels, shards(): pl.pallas_call(kernel, name='listwise', out_shape=(jax.ShapeDtypeStruct((...  51.5 us
    unnamed x3, local copies, waits for them, and re-layouts  1.76 us

profile of v2, /device:TPU:1, one launch (start us, length us, event | category | flops | bytes accessed | tf_op | source)
XLA Modules:
  0.0 53.9 jit_solution(9958841795370586422)
XLA Ops:
  0.6 51.5 %listwise.1 = (bf16[128,256]{1,0:T(8,128)(2,1)S(1)}, bf16[128,128]{1,0:T(8,128)(2,1)S(1)}, f32[1,128]{1,0:T(1,128)S(1)}) custom-call(bf16[128,4096]{1,0:T(8,128)(2,1)} %q_hbm.1, s32[128,128]{1,0:T(8,128)} %cand_hbm.1, s32[128,128]{1,0:T(8,128)} %teach_hbm.1, bf16[128,128]{1,0:T(8,128)(2,1)} %hid_hbm.1, bf16[1,128]{1,0:T(2,128)(2,1)} %bitcast.3), custom_call_target="tpu_custom_call" | custom-call | tf_op jit(solution)/shard_map/listwise/pallas_call | solution.py:381
  52.2 0.6 %copy.11 = bf16[128,256]{1,0:T(8,128)(2,1)} copy(bf16[128,256]{1,0:T(8,128)(2,1)S(1)} %get-tuple-element.12) | data formatting | bytes 131072
  52.8 0.6 %copy.12 = bf16[128,128]{1,0:T(8,128)(2,1)} copy(bf16[128,128]{1,0:T(8,128)(2,1)S(1)} %get-tuple-element.13) | data formatting | bytes 65536
  53.4 0.5 copy.13

commit v3 on v2

--- a/solution.py
+++ b/solution.py
@@ -9,6 +9,7 @@
 MESH = pl.DeviceIdType.MESH
 F32, BF16, I32 = jnp.float32, jnp.bfloat16, jnp.int32
 FAR_FIRST = (10, 6, 9, 11, 14, 2, 8, 5, 7, 13, 15, 1, 3, 4, 12)
+NEAR_Z = (4, 12, 3, 13, 2, 14, 1, 15)
 FAR_Z = (8, 7, 9, 6, 10, 5, 11, 4, 12, 3, 13, 2, 14, 1, 15)
 NZ = 16
 NC = 16
@@ -24,10 +25,10 @@
     q_hbm, cand_hbm, teach_hbm, hid_hbm, gain_hbm,
     qg_ref, hg_ref, gg_ref,
     q_ref, cand_ref, teach_ref, hid_ref, gain_ref, in_sem,
-    hf, hid32, xp, xz, ez, emb, inv, invp, tgt, tgt_t, sg, stat_s, stat_r, sp_s, sp_r,
+    hf, hid32, xp, xz, ez, emb, cand_t, inv_at, inv_code, inv_t, inv, tgt, tgt_t, sg, stat_s, stat_r, sp_s, sp_r,
     lg_s, lg_r, gfull, embz, eb, e32, sib_r, gs, gm_r, s6_s, s6_r, z7_s, z7_r,
     s1_sem, s1_dir, s1_rel, small_sem, xz_sem, st_sem, sp_sem, lg_sem, ez_sem, ez_dir, ez_rel,
-    sib_sem, gm_sem, s6_sem, z7_sem,
+    sib_sem, gm_sem, s6_sem, z7_sem, far_sem,
 ):
     me = lax.axis_index("query")
     z = lax.axis_index("passage")
@@ -91,7 +92,8 @@
             barrier, inc=1, device_id={"query": lax.bitwise_and(me + d, 31)}, device_id_type=MESH
         )
 
-    z_loop(hail_z)
+    for d in NEAR_Z:
+        hail_z(d)
     each(1, 32, hail_plane)
 
     arguments[0].wait()
@@ -110,34 +112,47 @@
     t = jnp.exp(t - jnp.max(t, axis=1, keepdims=True))
     tgt[...] = t / jnp.sum(t, axis=1, keepdims=True)
 
-    lane = lax.broadcasted_iota(I32, (8, B), 1)
-    owned_id = lane + z * B
-    base = lax.shift_left(lax.shift_right_logical(lane, 3), 7) + lax.bitwise_and(lane, 7)
-
-    def own_inverse(g):
-        rows = [pl.ds(pl.multiple_of(g * 32 + 8 * k, 8), 8) for k in range(4)]
-        cands = [cand_ref[r, :] for r in rows]
-        accs = [jnp.full((8, B), -1, I32) for _ in rows]
-        for c in range(B):
-            for k in range(4):
-                accs[k] = jnp.where(cands[k][:, c : c + 1] == owned_id, c, accs[k])
-        for k in range(4):
-            invp[rows[k], :] = accs[k]
-
-    def full_inverse(g):
-        rows = pl.ds(pl.multiple_of(g * 8, 8), 8)
-        cand = cand_ref[rows, :]
-        accs = [jnp.full((8, B), -1, I32) for _ in range(NC)]
-        for c in range(B):
-            one = jnp.broadcast_to(cand[:, c : c + 1], (8, B))
-            for b in range(NC):
-                accs[b] = jnp.where(one == base + 8 * b, c, accs[b])
-        for b in range(NC):
-            inv[rows, b * B : (b + 1) * B] = accs[b]
-
-    each(0, 4, own_inverse)
-
-    pl.semaphore_wait(barrier, NZ - 1 + 31)
+    cand_t[...] = cand_ref[...].T
+    own_at = lax.broadcasted_iota(I32, (B, B), 0) + z * B
+
+    def own_step(k, acc):
+        for c in range(8):
+            acc = jnp.where(cand_t[pl.ds(8 * k + c, 1), :] == own_at, 8 * k + c, acc)
+        return acc
+
+    inv_own_t = lax.fori_loop(0, B // 8, own_step, jnp.full((B, B), -1, I32))
+    listed_t = inv_own_t >= 0
+    inv_own = inv_own_t.T
+
+    ids = cand_t[...]
+    place = lax.bitwise_and(lax.shift_right_logical(ids, 3), NC - 1)
+    inv_at[...] = lax.shift_left(lax.shift_right_logical(ids, 7), 3) + lax.bitwise_and(ids, 7)
+    code = lax.shift_left(
+        lax.broadcasted_iota(I32, (B, B), 0) + 1, 8 * lax.bitwise_and(place, 3)
+    )
+    for w in range(4):
+        inv_code[w] = jnp.where(lax.shift_right_logical(place, 2) == w, code, 0)
+
+    def half_inverse(h):
+        half = B // 2
+        at = lax.broadcasted_iota(I32, (half, B), 0) + half * h
+
+        def step(k, accs):
+            accs = list(accs)
+            for u in range(8):
+                row = pl.ds(8 * k + u, 1)
+                hit = inv_at[row, :] == at
+                for w in range(4):
+                    accs[w] = lax.bitwise_or(jnp.where(hit, inv_code[w, row, :], 0), accs[w])
+            return tuple(accs)
+
+        accs = lax.fori_loop(0, B // 8, step, tuple(jnp.zeros((half, B), I32) for _ in range(4)))
+        for w in range(4):
+            inv_t[w, half * h : half * (h + 1), :] = accs[w]
+
+    pl.semaphore_wait(barrier, 31 + len(NEAR_Z))
+    for d in (4, 12):
+        pl.semaphore_signal(far_sem, inc=1, device_id={"passage": z_at(d)}, device_id_type=MESH)
 
     def send_small(d):
         t = chip_at(d)
@@ -153,7 +168,9 @@
     send(own, own, s1_sem.at[1], s1_rel.at[0], sibling)
     plane_loop(send_hidden)
 
-    each(0, 4, full_inverse)
+    half_inverse(0)
+
+    pl.semaphore_wait(far_sem, 2)
 
     drain(xp.at[pl.ds(0, NC - 1)], small_sem.at[1])
     xz[z] = xp[z]
@@ -190,9 +207,6 @@
     scores_t = (
         lax.dot_general(emb[...], q_ref[...], (((1,), (1,)), ((), ())), preferred_element_type=F32) * scale
     )
-    inv_own = invp[...]
-    listed = inv_own >= 0
-    listed_t = listed.astype(F32).T > 0.0
     masked = jnp.where(listed_t, scores_t, -1e30)
     top = jnp.max(masked, axis=0, keepdims=True)
     weight = jnp.where(listed_t, jnp.exp(masked - top), 0.0)
@@ -221,25 +235,27 @@
 
     z_loop(send_sparse)
 
-    drain(xz.at[pl.ds(0, NZ - 1)], xz_sem.at[1])
-    ez[core, chip] = xz[...].reshape(B, B).astype(BF16)
-
-    def send_rows(d):
-        t = chip_at(d)
-        block = ez.at[core, chip]
-        send(block, block, ez_sem.at[0], ez_dir.at[chip], {"query": 2 * t + core})
-
-    own_rows = ez.at[core, chip]
-    send(own_rows, own_rows, ez_sem.at[1], ez_rel.at[0], sibling)
-    plane_loop(send_rows)
-
     for g in range(16):
         rows = slice(8 * g, 8 * g + 8)
         i = inv_own[rows, :]
         sg[rows, :] = jnp.where(i >= 0, lanes(tgt[rows, :], jnp.maximum(i, 0)), 0.0)
     tgt_t[...] = sg[...].T
 
-    each(4, 12, full_inverse)
+    half_inverse(1)
+    for w in range(4):
+        inv[w] = inv_t[w].T
+
+    drain(xz.at[pl.ds(0, NZ - 1)], xz_sem.at[1])
+    ez[core, chip] = xz[...].reshape(B, B).astype(BF16)
+
+    def send_rows(d):
+        t = chip_at(d)
+        block = ez.at[core, chip]
+        send(block, block, ez_sem.at[0], ez_dir.at[chip], {"query": 2 * t + core})
+
+    own_rows = ez.at[core, chip]
+    send(own_rows, own_rows, ez_sem.at[1], ez_rel.at[0], sibling)
+    plane_loop(send_rows)
 
     drain(stat_r.at[pl.ds(0, NZ - 1)], st_sem.at[1])
     tops = [stat_r[k, 0:1, :] for k in range(NZ)]
@@ -299,16 +315,6 @@
 
     plane_loop(send_grads)
 
-    def relay_rows(d):
-        f = chip_from(d)
-        block = ez.at[core, f]
-        drain(block, ez_dir.at[f])
-        send(block, block, ez_sem.at[1], ez_rel.at[0], sibling)
-
-    plane_loop(relay_rows)
-
-    each(12, 16, full_inverse)
-
     drain(gm_r.at[pl.ds(0, 31)], gm_sem.at[1])
     small = gm_r[0]
     for k in range(1, 32):
@@ -320,6 +326,15 @@
         send(z7_s, z7_r.at[z], z7_sem.at[0], z7_sem.at[1], {"passage": z_at(d)})
 
     z_loop(send_plane_gain)
+
+    def relay_rows(d):
+        f = chip_from(d)
+        block = ez.at[core, f]
+        drain(block, ez_dir.at[f])
+        send(block, block, ez_sem.at[1], ez_rel.at[0], sibling)
+
+    plane_loop(relay_rows)
+
 
     drain(ez.at[other], ez_rel.at[0])
     rms_rows = jnp.concatenate([stat_r[k, 2:3, :] for k in range(NZ)], axis=0)
@@ -338,8 +353,9 @@
             cols = slice(b * B, (b + 1) * B)
             two = []
             for k in (g, g + 1):
-                i = inv[8 * k : 8 * k + 8, cols]
-                two.append(jnp.where(i >= 0, lanes(lg_r[k], jnp.maximum(i, 0)), 0.0))
+                i = lax.shift_right_logical(inv[b // 4, 8 * k : 8 * k + 8, :], 8 * (b % 4))
+                i = lax.bitwise_and(i, 255)
+                two.append(jnp.where(i > 0, lanes(lg_r[k], jnp.maximum(i - 1, 0)), 0.0))
             gfull[8 * g : 8 * g + 16, cols] = jnp.concatenate(two, axis=0).astype(BF16)
     qg_ref[...] = jnp.dot(gfull[...], embz[...], preferred_element_type=F32).astype(BF16)
 
@@ -401,8 +417,11 @@
             pltpu.VMEM((NZ, 8, B), F32),
             pltpu.VMEM((2, NC, B, B), BF16),
             pltpu.VMEM((B, D), BF16),
-            pltpu.VMEM((B, NC * B), I32),
             pltpu.VMEM((B, B), I32),
+            pltpu.VMEM((B, B), I32),
+            pltpu.VMEM((4, B, B), I32),
+            pltpu.VMEM((4, B, B), I32),
+            pltpu.VMEM((4, B, B), I32),
             pltpu.VMEM((B, B), F32),
             pltpu.VMEM((B, B), F32),
             pltpu.VMEM((B, B), F32),
@@ -438,6 +457,7 @@
             two,
             two,
             two,
+            pltpu.SemaphoreType.REGULAR,
         ],
         compiler_params=pltpu.CompilerParams(
             collective_id=0, has_side_effects=True, vmem_limit_bytes=48 * 2**20

time: 54.2 us -> 49 us (0.904)
  Pallas kernels: 51.5 us -> 46 us
    pallas_call x1, Pallas kernels: 51.5 us -> 46 us  [shards(): pl.pallas_call(kernel, name='listwise', out_shape=(jax.ShapeDtypeStruct((...]
where the time goes in v3:
time: 49 us; the launch traced here: 48.4 us
  Pallas kernels  46 us (94%)
  local copies, waits for them, and re-layouts  1.76 us (4%)
  between operations  0.64 us (1%)
    pallas_call x1, Pallas kernels, shards(): pl.pallas_call(kernel, name='listwise', out_shape=(jax.ShapeDtypeStruct((...  46 us
    unnamed x3, local copies, waits for them, and re-layouts  1.76 us

profile of v3, /device:TPU:1, one launch (start us, length us, event | category | flops | bytes accessed | tf_op | source)
XLA Modules:
  0.0 48.4 jit_solution(10954163553031382414)
XLA Ops:
  0.6 46.0 %listwise.1 = (bf16[128,256]{1,0:T(8,128)(2,1)S(1)}, bf16[128,128]{1,0:T(8,128)(2,1)S(1)}, f32[1,128]{1,0:T(1,128)S(1)}) custom-call(bf16[128,4096]{1,0:T(8,128)(2,1)} %q_hbm.1, s32[128,128]{1,0:T(8,128)} %cand_hbm.1, s32[128,128]{1,0:T(8,128)} %teach_hbm.1, bf16[128,128]{1,0:T(8,128)(2,1)} %hid_hbm.1, bf16[1,128]{1,0:T(2,128)(2,1)} %bitcast.3), custom_call_target="tpu_custom_call" | custom-call | tf_op jit(solution)/shard_map/listwise/pallas_call | solution.py:397
  46.7 0.6 %copy.11 = bf16[128,256]{1,0:T(8,128)(2,1)} copy(bf16[128,256]{1,0:T(8,128)(2,1)S(1)} %get-tuple-element.12) | data formatting | bytes 131072
  47.3 0.6 %copy.12 = bf16[128,128]{1,0:T(8,128)(2,1)} copy(bf16[128,128]{1,0:T(8,128)(2,1)S(1)} %get-tuple-element.13) | data formatting | bytes 65536
  47.9 0.5 %copy.13 = f32[128]{0:T(128)} copy(f32[128]{0:T(128)S(1)} %bitcast.2) | data formatting | bytes 1024

commit v4 on v3

--- a/solution.py
+++ b/solution.py
@@ -14,7 +14,6 @@
 NZ = 16
 NC = 16
 B = 128
-X = 144
 
 
 def lanes(x, index):
@@ -25,7 +24,7 @@
     q_hbm, cand_hbm, teach_hbm, hid_hbm, gain_hbm,
     qg_ref, hg_ref, gg_ref,
     q_ref, cand_ref, teach_ref, hid_ref, gain_ref, in_sem,
-    hf, hid32, xp, xz, ez, emb, cand_t, inv_at, inv_code, inv_t, inv, tgt, tgt_t, sg, stat_s, stat_r, sp_s, sp_r,
+    hf, gains, gain_sem, gain_rel, hid32, xp, xz, ez, emb, cand_t, inv_at, inv_code, inv_t, inv, tgt, tgt_t, sg, stat_s, stat_r, sp_s, sp_r,
     lg_s, lg_r, gfull, embz, eb, e32, sib_r, gs, gm_r, s6_s, s6_r, z7_s, z7_r,
     s1_sem, s1_dir, s1_rel, small_sem, xz_sem, st_sem, sp_sem, lg_sem, ez_sem, ez_dir, ez_rel,
     sib_sem, gm_sem, s6_sem, z7_sem, far_sem,
@@ -88,20 +87,20 @@
         pl.semaphore_signal(barrier, inc=1, device_id={"passage": z_at(d)}, device_id_type=MESH)
 
     def hail_plane(d):
-        pl.semaphore_signal(
-            barrier, inc=1, device_id={"query": lax.bitwise_and(me + d, 31)}, device_id_type=MESH
-        )
+        for k in (core, other):
+            pl.semaphore_signal(barrier, inc=1, device_id={"query": 2 * chip_at(d) + k}, device_id_type=MESH)
 
     for d in NEAR_Z:
         hail_z(d)
-    each(1, 32, hail_plane)
+    plane_loop(hail_plane)
+    pl.semaphore_signal(barrier, inc=1, device_id=sibling, device_id_type=MESH)
 
     arguments[0].wait()
     arguments[1].wait()
     hid = hid_ref[...]
     gain_row = gain_ref[...].astype(F32)
-    hf[core, chip, 0:B, :] = hid
-    hf[core, chip, B:X, :] = jnp.broadcast_to(gain_row, (16, B)).astype(BF16)
+    hf[core, chip] = hid
+    gains[core, chip] = gain_row
     h32 = hid.astype(F32)
     hid32[...] = h32.reshape(NC, 8, B)
     xp[chip] = hid32[chip]
@@ -164,10 +163,22 @@
         send(block, block, s1_sem.at[0], s1_dir.at[chip], {"query": 2 * t + core})
 
     plane_loop(send_small)
+
+    def send_own_gain(d):
+        t = chip_at(d)
+        row = gains.at[core, chip]
+        send(row, row, gain_sem.at[0], gain_sem.at[1], {"query": 2 * t + core})
+
+    plane_loop(send_own_gain)
     own = hf.at[core, chip]
     send(own, own, s1_sem.at[1], s1_rel.at[0], sibling)
     plane_loop(send_hidden)
 
+    for g in range(16):
+        rows = slice(8 * g, 8 * g + 8)
+        i = inv_own[rows, :]
+        sg[rows, :] = jnp.where(i >= 0, lanes(tgt[rows, :], jnp.maximum(i, 0)), 0.0)
+    tgt_t[...] = sg[...].T
     half_inverse(0)
 
     pl.semaphore_wait(far_sem, 2)
@@ -180,6 +191,8 @@
         send(xp.at[t], xz.at[z], xz_sem.at[0], xz_sem.at[1], {"passage": t})
 
     z_loop(send_slice)
+    drain(gains.at[core, pl.ds(0, NC - 1)], gain_sem.at[1])
+    send(gains.at[core], gains.at[core], gain_rel.at[0], gain_rel.at[1], sibling)
 
     def relay_hidden(d):
         f = chip_from(d)
@@ -189,18 +202,18 @@
 
     plane_loop(relay_hidden)
     drain(hf.at[other], s1_rel.at[0])
+    drain(gains.at[other], gain_rel.at[1])
 
     total = jnp.zeros((B, B), F32)
     for c in range(NC):
         for k in range(2):
-            x = hf[k, c, 0:B, :].astype(F32)
+            x = hf[k, c].astype(F32)
             total = total + x * x
     inv_rms = lax.rsqrt(jnp.sum(total, axis=1, keepdims=True) / float(D) + 1e-05)
     for c in range(NC):
         for k in range(2):
-            x = hf[k, c, 0:B, :].astype(F32)
-            g = hf[k, c, B:X, :].astype(F32)[0:1, :]
-            emb[:, (2 * c + k) * B : (2 * c + k + 1) * B] = (x * inv_rms * g).astype(BF16)
+            x = hf[k, c].astype(F32)
+            emb[:, (2 * c + k) * B : (2 * c + k + 1) * B] = (x * inv_rms * gains[k, c]).astype(BF16)
     rms_row = jnp.broadcast_to(inv_rms, (B, B)).T[0:1, :]
     scale = float(D) ** -0.5
     arguments[4].wait()
@@ -211,9 +224,8 @@
     top = jnp.max(masked, axis=0, keepdims=True)
     weight = jnp.where(listed_t, jnp.exp(masked - top), 0.0)
     part = jnp.sum(weight, axis=0, keepdims=True)
-    stat_s[0:1, :] = top
-    stat_s[1:2, :] = part
-    stat_s[2:3, :] = rms_row
+    stat_s[0:1, :] = jnp.where(part > 0.0, top + jnp.log(part), -1e30)
+    stat_s[1:2, :] = rms_row
     stat_r[z] = stat_s[...]
 
     def send_stat(d):
@@ -235,16 +247,6 @@
 
     z_loop(send_sparse)
 
-    for g in range(16):
-        rows = slice(8 * g, 8 * g + 8)
-        i = inv_own[rows, :]
-        sg[rows, :] = jnp.where(i >= 0, lanes(tgt[rows, :], jnp.maximum(i, 0)), 0.0)
-    tgt_t[...] = sg[...].T
-
-    half_inverse(1)
-    for w in range(4):
-        inv[w] = inv_t[w].T
-
     drain(xz.at[pl.ds(0, NZ - 1)], xz_sem.at[1])
     ez[core, chip] = xz[...].reshape(B, B).astype(BF16)
 
@@ -259,13 +261,12 @@
 
     drain(stat_r.at[pl.ds(0, NZ - 1)], st_sem.at[1])
     tops = [stat_r[k, 0:1, :] for k in range(NZ)]
-    parts = [stat_r[k, 1:2, :] for k in range(NZ)]
     top_all = tops[0]
     for k in range(1, NZ):
         top_all = jnp.maximum(top_all, tops[k])
     norm = jnp.zeros((1, B), F32)
     for k in range(NZ):
-        norm = norm + parts[k] * jnp.exp(tops[k] - top_all)
+        norm = norm + jnp.exp(tops[k] - top_all)
     table_t = jnp.where(listed_t, jnp.exp(masked - top_all) / norm - tgt_t[...], 0.0).astype(BF16)
     row_dot = jnp.sum(table_t.astype(F32) * scores_t, axis=1, keepdims=True)
     row_dot_row = jnp.broadcast_to(row_dot, (B, B)).T[0:1, :]
@@ -275,7 +276,7 @@
             e = both[:, k * B : (k + 1) * B]
             e32[k, c] = e
             eb[k, c] = e.astype(BF16)
-            terms = e * hf[k, c, 0:B, :].astype(F32) * inv_rms
+            terms = e * hf[k, c].astype(F32) * inv_rms
             gs[2 * c + k, 0:1, :] = jnp.sum(terms, axis=0, keepdims=True)
             gs[2 * c + k, 1:2, :] = row_dot_row
     gm_r[me] = gs[me]
@@ -315,6 +316,11 @@
 
     plane_loop(send_grads)
 
+    half_inverse(1)
+    for w in range(4):
+        inv[w] = inv_t[w].T
+
+
     drain(gm_r.at[pl.ds(0, 31)], gm_sem.at[1])
     small = gm_r[0]
     for k in range(1, 32):
@@ -337,16 +343,15 @@
 
 
     drain(ez.at[other], ez_rel.at[0])
-    rms_rows = jnp.concatenate([stat_r[k, 2:3, :] for k in range(NZ)], axis=0)
+    rms_rows = jnp.concatenate([stat_r[k, 1:2, :] for k in range(NZ)], axis=0)
     rms_t = jnp.concatenate([rms_rows, jnp.zeros((B - NZ, B), F32)], axis=0).T
-    gains = [hf[k, z, B:X, :].astype(F32)[0:1, :] for k in range(2)]
     for c in range(NC):
         col = jnp.concatenate(
             [jnp.broadcast_to(rms_t[8 * c : 8 * c + 8, k : k + 1], (8, B)) for k in range(NZ)], axis=0
         )
         for k in range(2):
             raw = ez[k, c].astype(F32)
-            embz[c * B : (c + 1) * B, k * B : (k + 1) * B] = (raw * col * gains[k]).astype(BF16)
+            embz[c * B : (c + 1) * B, k * B : (k + 1) * B] = (raw * col * gains[k, z]).astype(BF16)
     drain(lg_r.at[pl.ds(0, NZ - 1)], lg_sem.at[1])
     for g in range(0, 16, 2):
         for b in range(NC):
@@ -378,6 +383,8 @@
     drain(xp.at[pl.ds(0, n)], small_sem.at[0])
     drain(hf.at[0, pl.ds(0, n)], s1_sem.at[0])
     drain(hf.at[0], s1_sem.at[1])
+    drain(gains.at[0, pl.ds(0, n)], gain_sem.at[0])
+    drain(gains.at[0], gain_rel.at[0])
     drain(xz.at[pl.ds(0, n)], xz_sem.at[0])
     drain(stat_r.at[pl.ds(0, n)], st_sem.at[0])
     drain(sp_r.at[pl.ds(0, n)], sp_sem.at[0])
@@ -411,7 +418,10 @@
             pltpu.VMEM((B, B), BF16),
             pltpu.VMEM((1, B), BF16),
             pltpu.SemaphoreType.DMA((5,)),
-            pltpu.VMEM((2, NC, X, B), BF16),
+            pltpu.VMEM((2, NC, B, B), BF16),
+            pltpu.VMEM((2, NC, 1, B), F32),
+            two,
+            two,
             pltpu.VMEM((NC, 8, B), F32),
             pltpu.VMEM((NC, 8, B), F32),
             pltpu.VMEM((NZ, 8, B), F32),
@@ -425,8 +435,8 @@
             pltpu.VMEM((B, B), F32),
             pltpu.VMEM((B, B), F32),
             pltpu.VMEM((B, B), F32),
-            pltpu.VMEM((4, B), F32),
-            pltpu.VMEM((NZ, 4, B), F32),
+            pltpu.VMEM((2, B), F32),
+            pltpu.VMEM((NZ, 2, B), F32),
             pltpu.VMEM((NZ, 8, B), F32),
             pltpu.VMEM((NZ, 8, B), F32),
             pltpu.VMEM((8, B), F32),

time: 49 us -> 47.4 us (0.967)
  Pallas kernels: 46 us -> 44.8 us
    pallas_call x1, Pallas kernels: 46 us -> 44.8 us  [shards(): pl.pallas_call(kernel, name='listwise', out_shape=(jax.ShapeDtypeStruct((...]
where the time goes in v4:
time: 47.4 us; the launch traced here: 47.2 us
  Pallas kernels  44.8 us (95%)
  local copies, waits for them, and re-layouts  1.76 us (4%)
  between operations  0.64 us (1%)
    pallas_call x1, Pallas kernels, shards(): pl.pallas_call(kernel, name='listwise', out_shape=(jax.ShapeDtypeStruct((...  44.8 us
    unnamed x3, local copies, waits for them, and re-layouts  1.76 us

profile of v4, /device:TPU:1, one launch (start us, length us, event | category | flops | bytes accessed | tf_op | source)
XLA Modules:
  0.0 47.2 jit_solution(16293418218678573179)
XLA Ops:
  0.6 44.8 %listwise.1 = (bf16[128,256]{1,0:T(8,128)(2,1)S(1)}, bf16[128,128]{1,0:T(8,128)(2,1)S(1)}, f32[1,128]{1,0:T(1,128)S(1)}) custom-call(bf16[128,4096]{1,0:T(8,128)(2,1)} %q_hbm.1, s32[128,128]{1,0:T(8,128)} %cand_hbm.1, s32[128,128]{1,0:T(8,128)} %teach_hbm.1, bf16[128,128]{1,0:T(8,128)(2,1)} %hid_hbm.1, bf16[1,128]{1,0:T(2,128)(2,1)} %bitcast.3), custom_call_target="tpu_custom_call" | custom-call | tf_op jit(solution)/shard_map/listwise/pallas_call | solution.py:404
  45.5 0.6 %copy.11 = bf16[128,256]{1,0:T(8,128)(2,1)} copy(bf16[128,256]{1,0:T(8,128)(2,1)S(1)} %get-tuple-element.12) | data formatting | bytes 131072
  46.1 0.6 %copy.12 = bf16[128,128]{1,0:T(8,128)(2,1)} copy(bf16[128,128]{1,0:T(8,128)(2,1)S(1)} %get-tuple-element.13) | data formatting | bytes 65536
  46.7 0.5 %copy.13 = f32[128]{0:T(128)} copy(f32[128]{0:T(128)S(1)} %bitcast.2) | data formatting | bytes 1024

commit v5 on v4

--- a/solution.py
+++ b/solution.py
@@ -200,15 +200,18 @@
         drain(block, s1_dir.at[f])
         send(block, block, s1_sem.at[1], s1_rel.at[0], sibling)
 
-    plane_loop(relay_hidden)
+    mine = hf[core, chip].astype(F32)
+    total = mine * mine
+    for d in FAR_FIRST:
+        relay_hidden(d)
+        block = hf[core, chip_from(d)].astype(F32)
+        total = total + block * block
     drain(hf.at[other], s1_rel.at[0])
     drain(gains.at[other], gain_rel.at[1])
 
-    total = jnp.zeros((B, B), F32)
     for c in range(NC):
-        for k in range(2):
-            x = hf[k, c].astype(F32)
-            total = total + x * x
+        block = hf[other, c].astype(F32)
+        total = total + block * block
     inv_rms = lax.rsqrt(jnp.sum(total, axis=1, keepdims=True) / float(D) + 1e-05)
     for c in range(NC):
         for k in range(2):

time: 47.4 us -> 47.3 us (level)
  no operation moved by 1% of the time
where the time goes in v5:
time: 47.3 us; the launch traced here: 47.1 us
  Pallas kernels  44.8 us (95%)
  local copies, waits for them, and re-layouts  1.76 us (4%)
  between operations  0.64 us (1%)
    pallas_call x1, Pallas kernels, shards(): pl.pallas_call(kernel, name='listwise', out_shape=(jax.ShapeDtypeStruct((...  44.8 us
    unnamed x3, local copies, waits for them, and re-layouts  1.76 us

profile of v5, /device:TPU:1, one launch (start us, length us, event | category | flops | bytes accessed | tf_op | source)
XLA Modules:
  0.0 47.1 jit_solution(4842775409812186526)
XLA Ops:
  0.6 44.8 %listwise.1 = (bf16[128,256]{1,0:T(8,128)(2,1)S(1)}, bf16[128,128]{1,0:T(8,128)(2,1)S(1)}, f32[1,128]{1,0:T(1,128)S(1)}) custom-call(bf16[128,4096]{1,0:T(8,128)(2,1)} %q_hbm.1, s32[128,128]{1,0:T(8,128)} %cand_hbm.1, s32[128,128]{1,0:T(8,128)} %teach_hbm.1, bf16[128,128]{1,0:T(8,128)(2,1)} %hid_hbm.1, bf16[1,128]{1,0:T(2,128)(2,1)} %bitcast.3), custom_call_target="tpu_custom_call" | custom-call | tf_op jit(solution)/shard_map/listwise/pallas_call | solution.py:407
  45.4 0.6 %copy.11 = bf16[128,256]{1,0:T(8,128)(2,1)} copy(bf16[128,256]{1,0:T(8,128)(2,1)S(1)} %get-tuple-element.12) | data formatting | bytes 131072
  46.0 0.6 %copy.12 = bf16[128,128]{1,0:T(8,128)(2,1)} copy(bf16[128,128]{1,0:T(8,128)(2,1)S(1)} %get-tuple-element.13) | data formatting | bytes 65536
  46.6 0.5 %copy.13 = f32[128]{0:T(128)} copy(f32[128]{0:T(128)S(1)} %bitcast.2) | data formatting | bytes 1024
